TPU v7x, 128 devices: a whole 4x4x4 slice. The times are simulated.
128 devices in a mesh: grp: 4 (over x), row: 32 (over y, z, core).
Axes of the slice: x: 4, y: 4, z: 4, core: 2. Of those that a mesh axis runs over, the one named last changes fastest.
Arguments:
- matrix_tiles: float32 [512, 32, 128, 128], P(('grp', 'row')), may hold values from -2 to 2, as said below
- column_index: int32 [512, 32], P(('grp', 'row')), may hold values from 0 to 511, as said below
- precond: float32 [512, 128, 128], P(('grp', 'row')), may hold values from -12 to 16, as said below
- right_side: float32 [512, 16, 128], P(('grp', 'row')), may hold values from -60 to 60
- lost_group: int32 [1], replicated, may hold values from 0 to 16383
Outputs:
- recovered: float32 [512, 16, 128], P(('grp', 'row'))
- true_residual: float32 [512, 16, 128], P(('grp', 'row'))
Inputs may be any that keep to these rules, and one draw needn't show every extreme that they name: `column_index`: entry 0 of block row i is i; entry 1 is i + 12, or i - 12 where i + 12 passes the end; every entry lies within 12 of its block row. `precond`: every block is symmetric positive definite. `matrix_tiles`: the diagonal tile of each block row is near the identity.
All inputs are finite; a program needn't handle non-finite values.
Results may differ from a plain program's by a relative error of at most 0.0003.
Values sent between devices are 32-bit elements; how exact they have to be, the bound alone decides.
A program may use at most 64 MiB of HBM per device.

v0:
```python
import jax
import jax.numpy as jnp
from jax import lax
from jax.sharding import PartitionSpec as P

REACH = 3
OUTER = 2
INNER = 2
BAND = 12


def from_behind(value, axis, steps):
    count = lax.axis_size(axis)
    first, last = (max(0, -steps), min(count, count - steps))
    return lax.ppermute(value, axis, [(source, source + steps) for source in range(first, last)])


def inner_products(former, latter):
    return jnp.einsum("ica,ida->cd", former, latter, precision=lax.Precision.HIGHEST)


def scaled_by(vector, coeffs):
    return jnp.einsum("ica,cd->ida", vector, coeffs, precision=lax.Precision.HIGHEST)


def solve_sym(matrix, target):
    factor = jnp.linalg.cholesky(0.5 * (matrix + matrix.T))
    middle = lax.linalg.triangular_solve(factor, target, left_side=True, lower=True)
    return lax.linalg.triangular_solve(factor, middle, left_side=True, lower=True, transpose_a=True)


def neighbour(vector, offset):
    return from_behind(vector, ("grp", "row"), offset)


def group_neighbour(vector, offset):
    return from_behind(vector, "row", offset)


def window_of(vector, shifter):
    pieces = [shifter(vector, offset) for offset in range(REACH, 0, -1)]
    pieces.append(vector)
    for offset in range(1, REACH + 1):
        pieces.append(shifter(vector, -offset))
    return jnp.concatenate(pieces, 0)


def tile_product(matrix_tiles, window, local_cols, kept_mask):
    picked = jnp.take(window, local_cols, axis=0)
    if kept_mask is not None:
        picked = picked * kept_mask[:, :, None, None]
    return jnp.einsum("ikab,ikcb->ica", matrix_tiles, picked, precision=lax.Precision.HIGHEST)


def per_device(matrix_tiles, column_index, precond, right_side, lost_group):
    blocks = right_side.shape[0]
    row_count = lax.axis_size("row")
    group_count = lax.axis_size("grp")
    group_blocks = blocks * row_count
    my_group = lax.axis_index("grp")
    my_start = lax.axis_index(("grp", "row")) * blocks
    local_cols = column_index - (my_start - BAND)
    other_mask = (column_index // group_blocks != my_group).astype(jnp.float32)
    own_mask = 1.0 - other_mask
    lost = lost_group[0] % group_count

    def full_product(vector):
        return tile_product(matrix_tiles, window_of(vector, neighbour), local_cols, None)

    solution = jnp.zeros_like(right_side)
    residual = right_side
    direction = right_side
    squares = lax.psum(inner_products(residual, residual), ("grp", "row"))
    for outer_step in range(OUTER):
        applied = full_product(direction)
        curvature = lax.psum(inner_products(direction, applied), ("grp", "row"))
        advance = solve_sym(curvature, squares)
        solution = solution + scaled_by(direction, advance)
        residual = residual - scaled_by(applied, advance)
        squares_next = lax.psum(inner_products(residual, residual), ("grp", "row"))
        mixing = solve_sym(squares, squares_next)
        direction = residual + scaled_by(direction, mixing)
        squares = squares_next
    coupled = tile_product(matrix_tiles, window_of(solution, neighbour), local_cols, other_mask)
    inner_target = right_side - coupled

    def condition(vector):
        return jnp.einsum("iab,icb->ica", precond, vector, precision=lax.Precision.HIGHEST)

    estimate = jnp.zeros_like(inner_target)
    remainder = inner_target
    smoothed = condition(remainder)
    heading = smoothed
    weight = lax.psum(inner_products(remainder, smoothed), "row")
    for inner_step in range(INNER):
        applied = tile_product(
            matrix_tiles, window_of(heading, group_neighbour), local_cols, own_mask
        )
        bending = lax.psum(inner_products(heading, applied), "row")
        advance = solve_sym(bending, weight)
        estimate = estimate + scaled_by(heading, advance)
        remainder = remainder - scaled_by(applied, advance)
        if inner_step + 1 < INNER:
            smoothed = condition(remainder)
            weight_next = lax.psum(inner_products(remainder, smoothed), "row")
            heading = smoothed + scaled_by(heading, solve_sym(weight, weight_next))
            weight = weight_next
    recovered = jnp.where(my_group == lost, estimate, solution)
    true_residual = right_side - full_product(recovered)
    return (recovered, true_residual)


def solution(mesh):
    in_specs = (
        P(("grp", "row"), None, None, None),
        P(("grp", "row"), None),
        P(("grp", "row"), None, None),
        P(("grp", "row"), None, None),
        P(),
    )
    out_specs = (P(("grp", "row"), None, None), P(("grp", "row"), None, None))
    return jax.shard_map(
        per_device, mesh=mesh, in_specs=in_specs, out_specs=out_specs, check_vma=False
    )
```

profile of v0, /device:TPU:3, one launch (start us, length us, event | category | flops | bytes accessed | tf_op | source)
XLA Modules:
  0.0 685.8 jit_solution(15861666429005932232)
XLA Ops:
  0.6 8.8 %collective-permute-start.5 = (f32[4,16,128]{2,1,0:T(8,128)}, f32[4,16,128]{2,1,0:T(8,128)S(1)}, u32[]{:S(2)}, u32[]{:S(2)}) collective-permute-start(f32[4,16,128]{2,1,0:T(8,128)} %param.15), channel_id=1, source_target_pairs={{3,0},{4,1},{5,2},{6,3},{7,4},{8,5},{9,6},{10,7},{11,8},{12,9},{13... | collective-permute-start | bytes 98312 | tf_op jit(solution)/shard_map/ppermute | solution.py:15
  9.4 2.0 collective-permute-start.4
  11.5 2.2 collective-permute-start.3
  13.7 3.4 collective-permute-start.2
  17.1 3.6 collective-permute-start
  22.4 4.3 collective-permute-done
  26.7 1.9 collective-permute-start.1
  28.7 7.4 %collective-permute-done.1 = f32[4,16,128]{2,1,0:T(8,128)S(1)} collective-permute-done((f32[4,16,128]{2,1,0:T(8,128)}, f32[4,16,128]{2,1,0:T(8,128)S(1)}, u32[]{:S(2)}, u32[]{:S(2)}) %collective-permute-start.1) | collective-permute-done | bytes 32800 | tf_op jit(solution)/shard_map/ppermute | solution.py:15
  37.7 9.4 %convolution_bitcast_fusion.9 = f32[4,16,128]{2,1,0:T(8,128)S(1)} fusion(f32[4,32,128,128]{3,2,1,0:T(8,128)} %param.12, f32[4,32,16,128]{3,2,1,0:T(8,128)S(1)} %bitcast.246, pred[4,32]{1,0:T(4,128)(4,1)S(1)} %get-tuple-element.12), kind=kOutput, calls=%fused_computation.26 | convolution fusion | flops 402915328 | bytes 9470080 | tf_op jit(solution)/shard_map/ikab,ikcb->ica/dot_general | solution.py:52
  47.2 62.8 %all-reduce = (f32[16,16]{1,0:T(8,128)S(1)}, f32[16,16]{1,0:T(8,128)S(1)}) all-reduce(f32[16,16]{1,0:T(8,128)S(1)} %convolution_bitcast_fusion.22, f32[16,16]{1,0:T(8,128)S(1)} %convolution_bitcast_fusion.23), channel_id=1, replica_groups=mesh['grp'=4,'row'=32] {'grp','row'}, use_global_device_ids=true, to_apply=%region_3.6 | all-reduce | flops 512 | bytes 4096 | tf_op jit(solution)/shard_map/psum | solution.py:73
  110.2 1.5 cholesky.115
  113.0 1.2 custom-call.21
  114.3 1.5 cholesky.104
  117.1 1.2 custom-call.19
  119.1 64.1 %psum.58 = f32[16,16]{1,0:T(8,128)S(1)} all-reduce(f32[16,16]{1,0:T(8,128)S(1)} %convolution_bitcast_fusion.20), channel_id=1, replica_groups=mesh['grp'=4,'row'=32] {'grp','row'}, use_global_device_ids=true, to_apply=%region_4.9 | all-reduce | flops 256 | bytes 2048 | tf_op jit(solution)/shard_map/psum | solution.py:80
  183.8 3.8 collective-permute-start.6
  187.8 5.9 collective-permute-start.11
  193.7 1.9 collective-permute-start.10
  195.7 3.0 collective-permute-start.9
  198.7 3.5 collective-permute-start.8
  202.2 2.4 collective-permute-start.7
  204.6 6.5 collective-permute-done.7
  212.0 9.4 %convolution_bitcast_fusion.6 = f32[4,16,128]{2,1,0:T(8,128)S(1)} fusion(f32[4,32,128,128]{3,2,1,0:T(8,128)} %param.12, f32[4,32,16,128]{3,2,1,0:T(8,128)S(1)} %bitcast.247, pred[4,32]{1,0:T(4,128)(4,1)S(1)} %get-tuple-element.12), kind=kOutput, calls=%fused_computation.21 | convolution fusion | flops 402915328 | bytes 9470080 | tf_op jit(solution)/shard_map/ikab,ikcb->ica/dot_general | solution.py:52
  221.5 62.4 %psum.59 = f32[16,16]{1,0:T(8,128)S(1)} all-reduce(f32[16,16]{1,0:T(8,128)S(1)} %convolution_bitcast_fusion.18), channel_id=1, replica_groups=mesh['grp'=4,'row'=32] {'grp','row'}, use_global_device_ids=true, to_apply=%region_5.10 | all-reduce | flops 256 | bytes 2048 | tf_op jit(solution)/shard_map/psum | solution.py:76
  284.1 1.5 cholesky.126
  286.8 1.2 custom-call.23
  288.7 3.5 collective-permute-start.12
  292.9 6.3 collective-permute-start.17
  299.2 2.8 collective-permute-start.16
  302.0 3.4 collective-permute-start.15
  305.4 2.1 collective-permute-start.14
  307.5 2.8 collective-permute-start.13
  310.3 6.1 collective-permute-done.13
  317.3 9.4 %fusion.5 = f32[4,16,128]{2,1,0:T(8,128)S(1)} fusion(f32[4,16,128]{2,1,0:T(8,128)S(1)} %copy-done.1, f32[4,32,128,128]{3,2,1,0:T(8,128)} %param.12, f32[4,32,16,128]{3,2,1,0:T(8,128)S(1)} %bitcast.242, f32[4,32]{1,0:T(4,128)S(1)} %get-tuple-element.11, pred[4,32]{1,0:T(4,128)(4,1)S(1)} %get-tuple-element.12), kind=kOutput, calls=%fused_computation.18 | convolution fusion | flops 403185664 | bytes 9503360 | tf_op jit(solution)/shard_map/ikab,ikcb->ica/dot_general | solution.py:52
  327.2 1.3 collective-permute-start.18
  328.7 1.3 collective-permute-start.23
  330.0 1.3 collective-permute-start.22
  331.3 3.4 collective-permute-start.21
  334.7 4.2 collective-permute-start.20
  338.9 4.0 collective-permute-start.19
  344.7 9.4 %convolution_bitcast_fusion.4 = f32[4,16,128]{2,1,0:T(8,128)S(1)} fusion(f32[4,32,128,128]{3,2,1,0:T(8,128)} %param.12, f32[4,32,16,128]{3,2,1,0:T(8,128)S(1)} %bitcast.243, f32[4,32]{1,0:T(4,128)S(1)} %get-tuple-element.10, pred[4,32]{1,0:T(4,128)(4,1)S(1)} %get-tuple-element.12), kind=kOutput, calls=%fused_computation.16 | convolution fusion | flops 403177472 | bytes 9470592 | tf_op jit(solution)/shard_map/ikab,ikcb->ica/dot_general | solution.py:52
  354.3 119.3 %all-reduce.1 = (f32[16,16]{1,0:T(8,128)S(1)}, f32[16,16]{1,0:T(8,128)S(1)}) all-reduce(f32[16,16]{1,0:T(8,128)S(1)} %convolution_bitcast_fusion.15, f32[16,16]{1,0:T(8,128)S(1)} %convolution_bitcast_fusion.16), channel_id=1, replica_groups=mesh['grp'=4,'row'=32] {'row'}, use_global_device_ids=true, to_apply=%region_7.12 | all-reduce | flops 512 | bytes 4096 | tf_op jit(solution)/shard_map/psum | solution.py:94
  473.7 1.5 cholesky.137
  476.5 1.2 custom-call.25
  478.5 1.5 cholesky.148
  481.3 1.2 custom-call.27
  483.2 68.7 %psum.62 = f32[16,16]{1,0:T(8,128)S(1)} all-reduce(f32[16,16]{1,0:T(8,128)S(1)} %convolution_bitcast_fusion.13), channel_id=1, replica_groups=mesh['grp'=4,'row'=32] {'row'}, use_global_device_ids=true, to_apply=%region_8.13 | all-reduce | flops 256 | bytes 2048 | tf_op jit(solution)/shard_map/psum | solution.py:105
  552.4 1.3 collective-permute-start.24
  553.9 1.3 collective-permute-start.29
  555.2 1.3 collective-permute-start.28
  556.5 2.6 collective-permute-start.27
  559.1 4.2 collective-permute-start.26
  563.3 4.2 collective-permute-start.25
  569.1 9.4 %convolution_bitcast_fusion.1 = f32[4,16,128]{2,1,0:T(8,128)S(1)} fusion(f32[4,32,128,128]{3,2,1,0:T(8,128)} %param.12, f32[4,32,16,128]{3,2,1,0:T(8,128)S(1)} %bitcast.244, f32[4,32]{1,0:T(4,128)S(1)} %get-tuple-element.10, pred[4,32]{1,0:T(4,128)(4,1)S(1)} %get-tuple-element.12), kind=kOutput, calls=%fused_computation.11 | convolution fusion | flops 403177472 | bytes 9470592 | tf_op jit(solution)/shard_map/ikab,ikcb->ica/dot_general | solution.py:52
  578.7 62.6 %psum.63 = f32[16,16]{1,0:T(8,128)S(1)} all-reduce(f32[16,16]{1,0:T(8,128)S(1)} %convolution_bitcast_fusion.11), channel_id=1, replica_groups=mesh['grp'=4,'row'=32] {'row'}, use_global_device_ids=true, to_apply=%region_9.14 | all-reduce | flops 256 | bytes 2048 | tf_op jit(solution)/shard_map/psum | solution.py:99
  641.5 1.5 cholesky.159
  646.1 1.9 collective-permute-start.30
  648.1 7.9 %collective-permute-start.35 = (f32[4,16,128]{2,1,0:T(8,128)S(1)}, f32[4,16,128]{2,1,0:T(8,128)S(1)}, u32[]{:S(2)}, u32[]{:S(2)}) collective-permute-start(f32[4,16,128]{2,1,0:T(8,128)S(1)} %fusion.2), channel_id=1, source_target_pairs={{3,0},{4,1},{5,2},{6,3},{7,4},{8,5},{9,6},{10,7},{11,8},{12,9},{13... | collective-permute-start | bytes 98312 | tf_op jit(solution)/shard_map/ppermute | solution.py:15
  655.9 1.9 collective-permute-start.34
  657.9 4.7 collective-permute-start.33
  662.5 3.5 collective-permute-start.32
  666.1 2.0 collective-permute-start.31
  668.1 6.8 collective-permute-done.31
  675.8 10.0 %fusion = f32[4,16,128]{2,1,0:T(8,128)} fusion(f32[4,16,128]{2,1,0:T(8,128)S(1)} %copy-done.1, f32[4,32,128,128]{3,2,1,0:T(8,128)} %param.12, f32[4,32,16,128]{3,2,1,0:T(8,128)S(1)} %bitcast.245, pred[4,32]{1,0:T(4,128)(4,1)S(1)} %get-tuple-element.12), kind=kOutput, calls=%fused_computation.7 | convolution fusion | flops 402923520 | bytes 9502848 | tf_op jit(solution)/shard_map/ikab,ikcb->ica/dot_general | solution.py:52
  (163 shorter events, 25.1 us)
Async XLA Ops:
  0.6 326.1 %copy-start = (f32[4,128,128]{2,1,0:T(8,128)S(1)}, f32[4,128,128]{2,1,0:T(8,128)}, u32[]{:S(2)}) copy-start(f32[4,128,128]{2,1,0:T(8,128)} %param.14) | copy-start | bytes 786436
  0.6 36.2 %collective-permute-start.5 = (f32[4,16,128]{2,1,0:T(8,128)}, f32[4,16,128]{2,1,0:T(8,128)S(1)}, u32[]{:S(2)}, u32[]{:S(2)}) collective-permute-start(f32[4,16,128]{2,1,0:T(8,128)} %param.15), channel_id=1, source_target_pairs={{3,0},{4,1},{5,2},{6,3},{7,4},{8,5},{9,6},{10,7},{11,8},{12,9},{13... | collective-permute-start | bytes 98312 | tf_op jit(solution)/shard_map/ppermute | solution.py:15
  9.4 27.4 %collective-permute-start.4 = (f32[4,16,128]{2,1,0:T(8,128)}, f32[4,16,128]{2,1,0:T(8,128)S(1)}, u32[]{:S(2)}, u32[]{:S(2)}) collective-permute-start(f32[4,16,128]{2,1,0:T(8,128)} %param.15), channel_id=1, source_target_pairs={{2,0},{3,1},{4,2},{5,3},{6,4},{7,5},{8,6},{9,7},{10,8},{11,9},{12,... | collective-permute-start | bytes 98312 | tf_op jit(solution)/shard_map/ppermute | solution.py:15
  11.5 25.4 %collective-permute-start.3 = (f32[4,16,128]{2,1,0:T(8,128)}, f32[4,16,128]{2,1,0:T(8,128)S(1)}, u32[]{:S(2)}, u32[]{:S(2)}) collective-permute-start(f32[4,16,128]{2,1,0:T(8,128)} %param.15), channel_id=1, source_target_pairs={{1,0},{2,1},{3,2},{4,3},{5,4},{6,5},{7,6},{8,7},{9,8},{10,9},{11,1... | collective-permute-start | bytes 98312 | tf_op jit(solution)/shard_map/ppermute | solution.py:15
  13.7 22.4 %collective-permute-start.2 = (f32[4,16,128]{2,1,0:T(8,128)}, f32[4,16,128]{2,1,0:T(8,128)S(1)}, u32[]{:S(2)}, u32[]{:S(2)}) collective-permute-start(f32[4,16,128]{2,1,0:T(8,128)} %param.15), channel_id=1, source_target_pairs={{0,1},{1,2},{2,3},{3,4},{4,5},{5,6},{6,7},{7,8},{8,9},{9,10},{10,1... | collective-permute-start | bytes 98312 | tf_op jit(solution)/shard_map/ppermute | solution.py:15
  17.1 9.7 %collective-permute-start = (f32[4,16,128]{2,1,0:T(8,128)}, f32[4,16,128]{2,1,0:T(8,128)S(1)}, u32[]{:S(2)}, u32[]{:S(2)}) collective-permute-start(f32[4,16,128]{2,1,0:T(8,128)} %param.15), channel_id=1, source_target_pairs={{0,3},{1,4},{2,5},{3,6},{4,7},{5,8},{6,9},{7,10},{8,11},{9,12},{10... | collective-permute-start | bytes 98312 | tf_op jit(solution)/shard_map/ppermute | solution.py:15
  21.6 25.4 %copy-start.1 = (f32[4,16,128]{2,1,0:T(8,128)S(1)}, f32[4,16,128]{2,1,0:T(8,128)}, u32[]{:S(2)}) copy-start(f32[4,16,128]{2,1,0:T(8,128)} %param.15) | copy-start | bytes 98308
  26.7 9.3 %collective-permute-start.1 = (f32[4,16,128]{2,1,0:T(8,128)}, f32[4,16,128]{2,1,0:T(8,128)S(1)}, u32[]{:S(2)}, u32[]{:S(2)}) collective-permute-start(f32[4,16,128]{2,1,0:T(8,128)} %param.15), channel_id=1, source_target_pairs={{0,2},{1,3},{2,4},{3,5},{4,6},{5,7},{6,8},{7,9},{8,10},{9,11},{10,... | collective-permute-start | bytes 98312 | tf_op jit(solution)/shard_map/ppermute | solution.py:15
  183.8 18.4 %collective-permute-start.6 = (f32[4,16,128]{2,1,0:T(8,128)S(1)}, f32[4,16,128]{2,1,0:T(8,128)S(1)}, u32[]{:S(2)}, u32[]{:S(2)}) collective-permute-start(f32[4,16,128]{2,1,0:T(8,128)S(1)} %fusion.7), channel_id=1, source_target_pairs={{0,3},{1,4},{2,5},{3,6},{4,7},{5,8},{6,9},{7,10},{8,11},{9,12},{10... | collective-permute-start | bytes 98312 | tf_op jit(solution)/shard_map/ppermute | solution.py:15
  187.8 23.4 %collective-permute-start.11 = (f32[4,16,128]{2,1,0:T(8,128)S(1)}, f32[4,16,128]{2,1,0:T(8,128)S(1)}, u32[]{:S(2)}, u32[]{:S(2)}) collective-permute-start(f32[4,16,128]{2,1,0:T(8,128)S(1)} %fusion.7), channel_id=1, source_target_pairs={{3,0},{4,1},{5,2},{6,3},{7,4},{8,5},{9,6},{10,7},{11,8},{12,9},{13... | collective-permute-start | bytes 98312 | tf_op jit(solution)/shard_map/ppermute | solution.py:15
  193.7 17.4 %collective-permute-start.10 = (f32[4,16,128]{2,1,0:T(8,128)S(1)}, f32[4,16,128]{2,1,0:T(8,128)S(1)}, u32[]{:S(2)}, u32[]{:S(2)}) collective-permute-start(f32[4,16,128]{2,1,0:T(8,128)S(1)} %fusion.7), channel_id=1, source_target_pairs={{2,0},{3,1},{4,2},{5,3},{6,4},{7,5},{8,6},{9,7},{10,8},{11,9},{12,... | collective-permute-start | bytes 98312 | tf_op jit(solution)/shard_map/ppermute | solution.py:15
  195.7 15.5 %collective-permute-start.9 = (f32[4,16,128]{2,1,0:T(8,128)S(1)}, f32[4,16,128]{2,1,0:T(8,128)S(1)}, u32[]{:S(2)}, u32[]{:S(2)}) collective-permute-start(f32[4,16,128]{2,1,0:T(8,128)S(1)} %fusion.7), channel_id=1, source_target_pairs={{1,0},{2,1},{3,2},{4,3},{5,4},{6,5},{7,6},{8,7},{9,8},{10,9},{11,1... | collective-permute-start | bytes 98312 | tf_op jit(solution)/shard_map/ppermute | solution.py:15
  198.7 12.4 %collective-permute-start.8 = (f32[4,16,128]{2,1,0:T(8,128)S(1)}, f32[4,16,128]{2,1,0:T(8,128)S(1)}, u32[]{:S(2)}, u32[]{:S(2)}) collective-permute-start(f32[4,16,128]{2,1,0:T(8,128)S(1)} %fusion.7), channel_id=1, source_target_pairs={{0,1},{1,2},{2,3},{3,4},{4,5},{5,6},{6,7},{7,8},{8,9},{9,10},{10,1... | collective-permute-start | bytes 98312 | tf_op jit(solution)/shard_map/ppermute | solution.py:15
  202.2 8.9 %collective-permute-start.7 = (f32[4,16,128]{2,1,0:T(8,128)S(1)}, f32[4,16,128]{2,1,0:T(8,128)S(1)}, u32[]{:S(2)}, u32[]{:S(2)}) collective-permute-start(f32[4,16,128]{2,1,0:T(8,128)S(1)} %fusion.7), channel_id=1, source_target_pairs={{0,2},{1,3},{2,4},{3,5},{4,6},{5,7},{6,8},{7,9},{8,10},{9,11},{10,... | collective-permute-start | bytes 98312 | tf_op jit(solution)/shard_map/ppermute | solution.py:15
  211.2 81.0 %copy-start.3 = (s32[4,32]{1,0:T(4,128)S(1)}, s32[4,32]{1,0:T(4,128)}, u32[]{:S(2)}) copy-start(s32[4,32]{1,0:T(4,128)} %param.13) | copy-start | bytes 1540
  288.7 18.9 %collective-permute-start.12 = (f32[4,16,128]{2,1,0:T(8,128)S(1)}, f32[4,16,128]{2,1,0:T(8,128)S(1)}, u32[]{:S(2)}, u32[]{:S(2)}) collective-permute-start(f32[4,16,128]{2,1,0:T(8,128)S(1)} %fusion.6), channel_id=1, source_target_pairs={{0,3},{1,4},{2,5},{3,6},{4,7},{5,8},{6,9},{7,10},{8,11},{9,12},{10... | collective-permute-start | bytes 98312 | tf_op jit(solution)/shard_map/ppermute | solution.py:15
  292.9 23.6 %collective-permute-start.17 = (f32[4,16,128]{2,1,0:T(8,128)S(1)}, f32[4,16,128]{2,1,0:T(8,128)S(1)}, u32[]{:S(2)}, u32[]{:S(2)}) collective-permute-start(f32[4,16,128]{2,1,0:T(8,128)S(1)} %fusion.6), channel_id=1, source_target_pairs={{3,0},{4,1},{5,2},{6,3},{7,4},{8,5},{9,6},{10,7},{11,8},{12,9},{13... | collective-permute-start | bytes 98312 | tf_op jit(solution)/shard_map/ppermute | solution.py:15
  299.2 17.3 %collective-permute-start.16 = (f32[4,16,128]{2,1,0:T(8,128)S(1)}, f32[4,16,128]{2,1,0:T(8,128)S(1)}, u32[]{:S(2)}, u32[]{:S(2)}) collective-permute-start(f32[4,16,128]{2,1,0:T(8,128)S(1)} %fusion.6), channel_id=1, source_target_pairs={{2,0},{3,1},{4,2},{5,3},{6,4},{7,5},{8,6},{9,7},{10,8},{11,9},{12,... | collective-permute-start | bytes 98312 | tf_op jit(solution)/shard_map/ppermute | solution.py:15
  302.0 14.5 %collective-permute-start.15 = (f32[4,16,128]{2,1,0:T(8,128)S(1)}, f32[4,16,128]{2,1,0:T(8,128)S(1)}, u32[]{:S(2)}, u32[]{:S(2)}) collective-permute-start(f32[4,16,128]{2,1,0:T(8,128)S(1)} %fusion.6), channel_id=1, source_target_pairs={{1,0},{2,1},{3,2},{4,3},{5,4},{6,5},{7,6},{8,7},{9,8},{10,9},{11,1... | collective-permute-start | bytes 98312 | tf_op jit(solution)/shard_map/ppermute | solution.py:15
  305.4 11.0 %collective-permute-start.14 = (f32[4,16,128]{2,1,0:T(8,128)S(1)}, f32[4,16,128]{2,1,0:T(8,128)S(1)}, u32[]{:S(2)}, u32[]{:S(2)}) collective-permute-start(f32[4,16,128]{2,1,0:T(8,128)S(1)} %fusion.6), channel_id=1, source_target_pairs={{0,1},{1,2},{2,3},{3,4},{4,5},{5,6},{6,7},{7,8},{8,9},{9,10},{10,1... | collective-permute-start | bytes 98312 | tf_op jit(solution)/shard_map/ppermute | solution.py:15
  307.5 8.9 %collective-permute-start.13 = (f32[4,16,128]{2,1,0:T(8,128)S(1)}, f32[4,16,128]{2,1,0:T(8,128)S(1)}, u32[]{:S(2)}, u32[]{:S(2)}) collective-permute-start(f32[4,16,128]{2,1,0:T(8,128)S(1)} %fusion.6), channel_id=1, source_target_pairs={{0,2},{1,3},{2,4},{3,5},{4,6},{5,7},{6,8},{7,9},{8,10},{9,11},{10,... | collective-permute-start | bytes 98312 | tf_op jit(solution)/shard_map/ppermute | solution.py:15
  327.2 11.6 %collective-permute-start.18 = (f32[4,16,128]{2,1,0:T(8,128)S(1)}, f32[4,16,128]{2,1,0:T(8,128)S(1)}, u32[]{:S(2)}, u32[]{:S(2)}) collective-permute-start(f32[4,16,128]{2,1,0:T(8,128)S(1)} %fusion.81), channel_id=1, source_target_pairs={{0,3},{1,4},{2,5},{3,6},{4,7},{5,8},{6,9},{7,10},{8,11},{9,12},{10... | collective-permute-start | bytes 98312 | tf_op jit(solution)/shard_map/ppermute | solution.py:15
  328.7 15.3 %collective-permute-start.23 = (f32[4,16,128]{2,1,0:T(8,128)S(1)}, f32[4,16,128]{2,1,0:T(8,128)S(1)}, u32[]{:S(2)}, u32[]{:S(2)}) collective-permute-start(f32[4,16,128]{2,1,0:T(8,128)S(1)} %fusion.81), channel_id=1, source_target_pairs={{3,0},{4,1},{5,2},{6,3},{7,4},{8,5},{9,6},{10,7},{11,8},{12,9},{13... | collective-permute-start | bytes 98312 | tf_op jit(solution)/shard_map/ppermute | solution.py:15
  330.0 13.9 %collective-permute-start.22 = (f32[4,16,128]{2,1,0:T(8,128)S(1)}, f32[4,16,128]{2,1,0:T(8,128)S(1)}, u32[]{:S(2)}, u32[]{:S(2)}) collective-permute-start(f32[4,16,128]{2,1,0:T(8,128)S(1)} %fusion.81), channel_id=1, source_target_pairs={{2,0},{3,1},{4,2},{5,3},{6,4},{7,5},{8,6},{9,7},{10,8},{11,9},{12,... | collective-permute-start | bytes 98312 | tf_op jit(solution)/shard_map/ppermute | solution.py:15
  331.3 12.6 %collective-permute-start.21 = (f32[4,16,128]{2,1,0:T(8,128)S(1)}, f32[4,16,128]{2,1,0:T(8,128)S(1)}, u32[]{:S(2)}, u32[]{:S(2)}) collective-permute-start(f32[4,16,128]{2,1,0:T(8,128)S(1)} %fusion.81), channel_id=1, source_target_pairs={{1,0},{2,1},{3,2},{4,3},{5,4},{6,5},{7,6},{8,7},{9,8},{10,9},{11,1... | collective-permute-start | bytes 98312 | tf_op jit(solution)/shard_map/ppermute | solution.py:15
  334.7 9.2 %collective-permute-start.20 = (f32[4,16,128]{2,1,0:T(8,128)S(1)}, f32[4,16,128]{2,1,0:T(8,128)S(1)}, u32[]{:S(2)}, u32[]{:S(2)}) collective-permute-start(f32[4,16,128]{2,1,0:T(8,128)S(1)} %fusion.81), channel_id=1, source_target_pairs={{0,1},{1,2},{2,3},{3,4},{4,5},{5,6},{6,7},{7,8},{8,9},{9,10},{10,1... | collective-permute-start | bytes 98312 | tf_op jit(solution)/shard_map/ppermute | solution.py:15
  338.9 5.0 collective-permute-start.19
  552.4 10.8 %collective-permute-start.24 = (f32[4,16,128]{2,1,0:T(8,128)S(1)}, f32[4,16,128]{2,1,0:T(8,128)S(1)}, u32[]{:S(2)}, u32[]{:S(2)}) collective-permute-start(f32[4,16,128]{2,1,0:T(8,128)S(1)} %fusion.3), channel_id=1, source_target_pairs={{0,3},{1,4},{2,5},{3,6},{4,7},{5,8},{6,9},{7,10},{8,11},{9,12},{10... | collective-permute-start | bytes 98312 | tf_op jit(solution)/shard_map/ppermute | solution.py:15
  553.9 14.5 %collective-permute-start.29 = (f32[4,16,128]{2,1,0:T(8,128)S(1)}, f32[4,16,128]{2,1,0:T(8,128)S(1)}, u32[]{:S(2)}, u32[]{:S(2)}) collective-permute-start(f32[4,16,128]{2,1,0:T(8,128)S(1)} %fusion.3), channel_id=1, source_target_pairs={{3,0},{4,1},{5,2},{6,3},{7,4},{8,5},{9,6},{10,7},{11,8},{12,9},{13... | collective-permute-start | bytes 98312 | tf_op jit(solution)/shard_map/ppermute | solution.py:15
  555.2 13.1 %collective-permute-start.28 = (f32[4,16,128]{2,1,0:T(8,128)S(1)}, f32[4,16,128]{2,1,0:T(8,128)S(1)}, u32[]{:S(2)}, u32[]{:S(2)}) collective-permute-start(f32[4,16,128]{2,1,0:T(8,128)S(1)} %fusion.3), channel_id=1, source_target_pairs={{2,0},{3,1},{4,2},{5,3},{6,4},{7,5},{8,6},{9,7},{10,8},{11,9},{12,... | collective-permute-start | bytes 98312 | tf_op jit(solution)/shard_map/ppermute | solution.py:15
  556.5 11.8 %collective-permute-start.27 = (f32[4,16,128]{2,1,0:T(8,128)S(1)}, f32[4,16,128]{2,1,0:T(8,128)S(1)}, u32[]{:S(2)}, u32[]{:S(2)}) collective-permute-start(f32[4,16,128]{2,1,0:T(8,128)S(1)} %fusion.3), channel_id=1, source_target_pairs={{1,0},{2,1},{3,2},{4,3},{5,4},{6,5},{7,6},{8,7},{9,8},{10,9},{11,1... | collective-permute-start | bytes 98312 | tf_op jit(solution)/shard_map/ppermute | solution.py:15
  559.1 9.2 %collective-permute-start.26 = (f32[4,16,128]{2,1,0:T(8,128)S(1)}, f32[4,16,128]{2,1,0:T(8,128)S(1)}, u32[]{:S(2)}, u32[]{:S(2)}) collective-permute-start(f32[4,16,128]{2,1,0:T(8,128)S(1)} %fusion.3), channel_id=1, source_target_pairs={{0,1},{1,2},{2,3},{3,4},{4,5},{5,6},{6,7},{7,8},{8,9},{9,10},{10,1... | collective-permute-start | bytes 98312 | tf_op jit(solution)/shard_map/ppermute | solution.py:15
  563.3 5.0 collective-permute-start.25
  646.1 39.7 %copy-start.2 = (f32[4,16,128]{2,1,0:T(8,128)}, f32[4,16,128]{2,1,0:T(8,128)S(1)}, u32[]{:S(2)}) copy-start(f32[4,16,128]{2,1,0:T(8,128)S(1)} %fusion.2) | copy-start | bytes 98308
  646.1 19.9 %collective-permute-start.30 = (f32[4,16,128]{2,1,0:T(8,128)S(1)}, f32[4,16,128]{2,1,0:T(8,128)S(1)}, u32[]{:S(2)}, u32[]{:S(2)}) collective-permute-start(f32[4,16,128]{2,1,0:T(8,128)S(1)} %fusion.2), channel_id=1, source_target_pairs={{0,3},{1,4},{2,5},{3,6},{4,7},{5,8},{6,9},{7,10},{8,11},{9,12},{10... | collective-permute-start | bytes 98312 | tf_op jit(solution)/shard_map/ppermute | solution.py:15
  648.1 27.0 %collective-permute-start.35 = (f32[4,16,128]{2,1,0:T(8,128)S(1)}, f32[4,16,128]{2,1,0:T(8,128)S(1)}, u32[]{:S(2)}, u32[]{:S(2)}) collective-permute-start(f32[4,16,128]{2,1,0:T(8,128)S(1)} %fusion.2), channel_id=1, source_target_pairs={{3,0},{4,1},{5,2},{6,3},{7,4},{8,5},{9,6},{10,7},{11,8},{12,9},{13... | collective-permute-start | bytes 98312 | tf_op jit(solution)/shard_map/ppermute | solution.py:15
  655.9 19.1 %collective-permute-start.34 = (f32[4,16,128]{2,1,0:T(8,128)S(1)}, f32[4,16,128]{2,1,0:T(8,128)S(1)}, u32[]{:S(2)}, u32[]{:S(2)}) collective-permute-start(f32[4,16,128]{2,1,0:T(8,128)S(1)} %fusion.2), channel_id=1, source_target_pairs={{2,0},{3,1},{4,2},{5,3},{6,4},{7,5},{8,6},{9,7},{10,8},{11,9},{12,... | collective-permute-start | bytes 98312 | tf_op jit(solution)/shard_map/ppermute | solution.py:15
  657.9 17.1 %collective-permute-start.33 = (f32[4,16,128]{2,1,0:T(8,128)S(1)}, f32[4,16,128]{2,1,0:T(8,128)S(1)}, u32[]{:S(2)}, u32[]{:S(2)}) collective-permute-start(f32[4,16,128]{2,1,0:T(8,128)S(1)} %fusion.2), channel_id=1, source_target_pairs={{1,0},{2,1},{3,2},{4,3},{5,4},{6,5},{7,6},{8,7},{9,8},{10,9},{11,1... | collective-permute-start | bytes 98312 | tf_op jit(solution)/shard_map/ppermute | solution.py:15
  662.5 12.4 %collective-permute-start.32 = (f32[4,16,128]{2,1,0:T(8,128)S(1)}, f32[4,16,128]{2,1,0:T(8,128)S(1)}, u32[]{:S(2)}, u32[]{:S(2)}) collective-permute-start(f32[4,16,128]{2,1,0:T(8,128)S(1)} %fusion.2), channel_id=1, source_target_pairs={{0,1},{1,2},{2,3},{3,4},{4,5},{5,6},{6,7},{7,8},{8,9},{9,10},{10,1... | collective-permute-start | bytes 98312 | tf_op jit(solution)/shard_map/ppermute | solution.py:15
  666.1 8.9 %collective-permute-start.31 = (f32[4,16,128]{2,1,0:T(8,128)S(1)}, f32[4,16,128]{2,1,0:T(8,128)S(1)}, u32[]{:S(2)}, u32[]{:S(2)}) collective-permute-start(f32[4,16,128]{2,1,0:T(8,128)S(1)} %fusion.2), channel_id=1, source_target_pairs={{0,2},{1,3},{2,4},{3,5},{4,6},{5,7},{6,8},{7,9},{8,10},{9,11},{10,... | collective-permute-start | bytes 98312 | tf_op jit(solution)/shard_map/ppermute | solution.py:15
where the time goes:
time: 687 us; the launch traced here: 686 us
  blocking collectives  440 us (64%)
  starting transfers between devices  116 us (17%)
  matrix products  63.8 us (9%)
  waiting for transfers between devices  32.9 us (5%)
  other arithmetic  24.9 us (4%)
    psum x1, blocking collectives, per_device(): weight = lax.psum(inner_products(remainder, smoothed), 'row')  119 us
    ppermute x36, starting transfers between devices, from_behind(): lax.ppermute(value, axis, [(source, source + steps) for source in range(f...  116 us
    psum x1, blocking collectives, per_device(): weight_next = lax.psum(inner_products(remainder, smoothed), 'row')  68.7 us
    psum x1, blocking collectives, per_device(): squares_next = lax.psum(inner_products(residual, residual), ('grp', 'row'))  64.1 us
    psum x1, blocking collectives, per_device(): squares = lax.psum(inner_products(residual, residual), ('grp', 'row'))  62.8 us
    psum x1, blocking collectives, per_device(): bending = lax.psum(inner_products(heading, applied), 'row')  62.6 us
    psum x1, blocking collectives, per_device(): curvature = lax.psum(inner_products(direction, applied), ('grp', 'row'))  62.4 us
    dot_general x6, matrix products, tile_product(): jnp.einsum('ikab,ikcb->ica', matrix_tiles, picked, precision=lax.Precisio...  57 us
  transfers between devices with their start and end apart: 36, of which 7 were waited for; matrix products, arithmetic and copies ran while one was open for 0% of the time, Pallas kernels for 0%

commit v1 on v0

--- a/solution.py
+++ b/solution.py
@@ -77,7 +77,7 @@
         advance = solve_sym(curvature, squares)
         solution = solution + scaled_by(direction, advance)
         residual = residual - scaled_by(applied, advance)
-        squares_next = lax.psum(inner_products(residual, residual), ("grp", "row"))
+        squares_next = lax.psum(lax.psum(inner_products(residual, residual), "row"), "grp")
         mixing = solve_sym(squares, squares_next)
         direction = residual + scaled_by(direction, mixing)
         squares = squares_next

time: 687 us -> 698 us (1.016)
  blocking collectives: 440 us -> 448 us
    psum x1 -> x2, blocking collectives: 64.1 us -> 72.3 us  [the longest x1 63.6 us: per_device(): lax.psum(inner_products(residual, residual), 'row')]
where the time goes in v1:
time: 698 us; the launch traced here: 697 us
  blocking collectives  448 us (64%)
  starting transfers between devices  118 us (17%)
  matrix products  63.8 us (9%)
  waiting for transfers between devices  34 us (5%)
  other arithmetic  24.9 us (4%)
    psum x1, blocking collectives, per_device(): weight = lax.psum(inner_products(remainder, smoothed), 'row')  120 us
    ppermute x36, starting transfers between devices, from_behind(): lax.ppermute(value, axis, [(source, source + steps) for source in range(f...  118 us
    psum x1, blocking collectives, per_device(): weight_next = lax.psum(inner_products(remainder, smoothed), 'row')  68.7 us
    psum x1, blocking collectives, per_device(): lax.psum(inner_products(residual, residual), 'row')  63.6 us
    psum x1, blocking collectives, per_device(): squares = lax.psum(inner_products(residual, residual), ('grp', 'row'))  62.8 us
    psum x1, blocking collectives, per_device(): bending = lax.psum(inner_products(heading, applied), 'row')  62.6 us
    psum x1, blocking collectives, per_device(): curvature = lax.psum(inner_products(direction, applied), ('grp', 'row'))  61.6 us
    dot_general x6, matrix products, tile_product(): jnp.einsum('ikab,ikcb->ica', matrix_tiles, picked, precision=lax.Precisio...  57 us
  transfers between devices with their start and end apart: 36, of which 7 were waited for; matrix products, arithmetic and copies ran while one was open for 0% of the time, Pallas kernels for 0%

profile of v1, /device:TPU:3, one launch (start us, length us, event | category | flops | bytes accessed | tf_op | source)
XLA Modules:
  0.0 696.8 jit_solution(6913116130054624612)
XLA Ops:
  0.6 8.8 %collective-permute-start.5 = (f32[4,16,128]{2,1,0:T(8,128)}, f32[4,16,128]{2,1,0:T(8,128)S(1)}, u32[]{:S(2)}, u32[]{:S(2)}) collective-permute-start(f32[4,16,128]{2,1,0:T(8,128)} %param.15), channel_id=1, source_target_pairs={{3,0},{4,1},{5,2},{6,3},{7,4},{8,5},{9,6},{10,7},{11,8},{12,9},{13... | collective-permute-start | bytes 98312 | tf_op jit(solution)/shard_map/ppermute | solution.py:15
  9.4 2.0 collective-permute-start.4
  11.5 2.2 collective-permute-start.3
  13.7 3.4 collective-permute-start.2
  17.1 3.6 collective-permute-start
  22.4 4.3 collective-permute-done
  26.7 1.9 collective-permute-start.1
  28.7 7.4 %collective-permute-done.1 = f32[4,16,128]{2,1,0:T(8,128)S(1)} collective-permute-done((f32[4,16,128]{2,1,0:T(8,128)}, f32[4,16,128]{2,1,0:T(8,128)S(1)}, u32[]{:S(2)}, u32[]{:S(2)}) %collective-permute-start.1) | collective-permute-done | bytes 32800 | tf_op jit(solution)/shard_map/ppermute | solution.py:15
  37.7 9.4 %convolution_bitcast_fusion.9 = f32[4,16,128]{2,1,0:T(8,128)S(1)} fusion(f32[4,32,128,128]{3,2,1,0:T(8,128)} %param.12, f32[4,32,16,128]{3,2,1,0:T(8,128)S(1)} %bitcast.246, pred[4,32]{1,0:T(4,128)(4,1)S(1)} %get-tuple-element.12), kind=kOutput, calls=%fused_computation.26 | convolution fusion | flops 402915328 | bytes 9470080 | tf_op jit(solution)/shard_map/ikab,ikcb->ica/dot_general | solution.py:52
  47.2 62.8 %all-reduce = (f32[16,16]{1,0:T(8,128)S(1)}, f32[16,16]{1,0:T(8,128)S(1)}) all-reduce(f32[16,16]{1,0:T(8,128)S(1)} %convolution_bitcast_fusion.22, f32[16,16]{1,0:T(8,128)S(1)} %convolution_bitcast_fusion.23), channel_id=1, replica_groups=mesh['grp'=4,'row'=32] {'grp','row'}, use_global_device_ids=true, to_apply=%region_3.6 | all-reduce | flops 512 | bytes 4096 | tf_op jit(solution)/shard_map/psum | solution.py:73
  110.2 1.5 cholesky.115
  113.0 1.2 custom-call.21
  114.3 1.5 cholesky.104
  117.1 1.2 custom-call.19
  119.1 63.6 %psum.65 = f32[16,16]{1,0:T(8,128)S(1)} all-reduce(f32[16,16]{1,0:T(8,128)S(1)} %convolution_bitcast_fusion.20), channel_id=1, replica_groups=mesh['grp'=4,'row'=32] {'row'}, use_global_device_ids=true, to_apply=%region_4.9 | all-reduce | flops 256 | bytes 2048 | tf_op jit(solution)/shard_map/psum | solution.py:80
  182.7 8.7 %psum.66 = f32[16,16]{1,0:T(8,128)S(1)} all-reduce(f32[16,16]{1,0:T(8,128)S(1)} %psum.65), channel_id=1, replica_groups=mesh['grp'=4,'row'=32] {'grp'}, use_global_device_ids=true, to_apply=%region_5.10 | all-reduce | flops 256 | bytes 2048 | tf_op jit(solution)/shard_map/psum | solution.py:80
  192.0 1.9 collective-permute-start.6
  194.1 7.9 %collective-permute-start.11 = (f32[4,16,128]{2,1,0:T(8,128)S(1)}, f32[4,16,128]{2,1,0:T(8,128)S(1)}, u32[]{:S(2)}, u32[]{:S(2)}) collective-permute-start(f32[4,16,128]{2,1,0:T(8,128)S(1)} %fusion.7), channel_id=1, source_target_pairs={{3,0},{4,1},{5,2},{6,3},{7,4},{8,5},{9,6},{10,7},{11,8},{12,9},{13... | collective-permute-start | bytes 98312 | tf_op jit(solution)/shard_map/ppermute | solution.py:15
  201.9 1.9 collective-permute-start.10
  203.9 6.5 collective-permute-start.9
  210.4 3.5 collective-permute-start.8
  214.0 2.0 collective-permute-start.7
  216.0 6.8 collective-permute-done.7
  223.7 9.4 %convolution_bitcast_fusion.6 = f32[4,16,128]{2,1,0:T(8,128)S(1)} fusion(f32[4,32,128,128]{3,2,1,0:T(8,128)} %param.12, f32[4,32,16,128]{3,2,1,0:T(8,128)S(1)} %bitcast.247, pred[4,32]{1,0:T(4,128)(4,1)S(1)} %get-tuple-element.12), kind=kOutput, calls=%fused_computation.21 | convolution fusion | flops 402915328 | bytes 9470080 | tf_op jit(solution)/shard_map/ikab,ikcb->ica/dot_general | solution.py:52
  233.3 61.6 %psum.67 = f32[16,16]{1,0:T(8,128)S(1)} all-reduce(f32[16,16]{1,0:T(8,128)S(1)} %convolution_bitcast_fusion.18), channel_id=1, replica_groups=mesh['grp'=4,'row'=32] {'grp','row'}, use_global_device_ids=true, to_apply=%region_6.11 | all-reduce | flops 256 | bytes 2048 | tf_op jit(solution)/shard_map/psum | solution.py:76
  295.0 1.5 cholesky.126
  297.8 1.2 custom-call.23
  299.7 3.6 collective-permute-start.12
  304.0 6.2 collective-permute-start.17
  310.1 2.5 collective-permute-start.16
  312.7 3.1 collective-permute-start.15
  315.8 2.7 collective-permute-start.14
  318.5 2.6 collective-permute-start.13
  321.0 6.8 collective-permute-done.13
  328.7 9.4 %fusion.5 = f32[4,16,128]{2,1,0:T(8,128)S(1)} fusion(f32[4,16,128]{2,1,0:T(8,128)S(1)} %copy-done.1, f32[4,32,128,128]{3,2,1,0:T(8,128)} %param.12, f32[4,32,16,128]{3,2,1,0:T(8,128)S(1)} %bitcast.242, f32[4,32]{1,0:T(4,128)S(1)} %get-tuple-element.11, pred[4,32]{1,0:T(4,128)(4,1)S(1)} %get-tuple-element.12), kind=kOutput, calls=%fused_computation.18 | convolution fusion | flops 403185664 | bytes 9503360 | tf_op jit(solution)/shard_map/ikab,ikcb->ica/dot_general | solution.py:52
  338.6 1.3 collective-permute-start.18
  340.1 1.3 collective-permute-start.23
  341.4 1.3 collective-permute-start.22
  342.7 2.5 collective-permute-start.21
  345.2 4.2 collective-permute-start.20
  349.4 4.0 collective-permute-start.19
  355.2 9.4 %convolution_bitcast_fusion.4 = f32[4,16,128]{2,1,0:T(8,128)S(1)} fusion(f32[4,32,128,128]{3,2,1,0:T(8,128)} %param.12, f32[4,32,16,128]{3,2,1,0:T(8,128)S(1)} %bitcast.243, f32[4,32]{1,0:T(4,128)S(1)} %get-tuple-element.10, pred[4,32]{1,0:T(4,128)(4,1)S(1)} %get-tuple-element.12), kind=kOutput, calls=%fused_computation.16 | convolution fusion | flops 403177472 | bytes 9470592 | tf_op jit(solution)/shard_map/ikab,ikcb->ica/dot_general | solution.py:52
  364.8 119.7 %all-reduce.1 = (f32[16,16]{1,0:T(8,128)S(1)}, f32[16,16]{1,0:T(8,128)S(1)}) all-reduce(f32[16,16]{1,0:T(8,128)S(1)} %convolution_bitcast_fusion.15, f32[16,16]{1,0:T(8,128)S(1)} %convolution_bitcast_fusion.16), channel_id=1, replica_groups=mesh['grp'=4,'row'=32] {'row'}, use_global_device_ids=true, to_apply=%region_8.13 | all-reduce | flops 512 | bytes 4096 | tf_op jit(solution)/shard_map/psum | solution.py:94
  484.7 1.5 cholesky.137
  487.5 1.2 custom-call.25
  489.5 1.5 cholesky.148
  494.2 68.7 %psum.70 = f32[16,16]{1,0:T(8,128)S(1)} all-reduce(f32[16,16]{1,0:T(8,128)S(1)} %convolution_bitcast_fusion.13), channel_id=1, replica_groups=mesh['grp'=4,'row'=32] {'row'}, use_global_device_ids=true, to_apply=%region_9.14 | all-reduce | flops 256 | bytes 2048 | tf_op jit(solution)/shard_map/psum | solution.py:105
  563.4 1.3 collective-permute-start.24
  564.9 1.3 collective-permute-start.29
  566.2 1.3 collective-permute-start.28
  567.5 2.6 collective-permute-start.27
  570.1 4.2 collective-permute-start.26
  574.3 4.2 collective-permute-start.25
  580.1 9.4 %convolution_bitcast_fusion.1 = f32[4,16,128]{2,1,0:T(8,128)S(1)} fusion(f32[4,32,128,128]{3,2,1,0:T(8,128)} %param.12, f32[4,32,16,128]{3,2,1,0:T(8,128)S(1)} %bitcast.244, f32[4,32]{1,0:T(4,128)S(1)} %get-tuple-element.10, pred[4,32]{1,0:T(4,128)(4,1)S(1)} %get-tuple-element.12), kind=kOutput, calls=%fused_computation.11 | convolution fusion | flops 403177472 | bytes 9470592 | tf_op jit(solution)/shard_map/ikab,ikcb->ica/dot_general | solution.py:52
  589.7 62.6 %psum.71 = f32[16,16]{1,0:T(8,128)S(1)} all-reduce(f32[16,16]{1,0:T(8,128)S(1)} %convolution_bitcast_fusion.11), channel_id=1, replica_groups=mesh['grp'=4,'row'=32] {'row'}, use_global_device_ids=true, to_apply=%region_10.15 | all-reduce | flops 256 | bytes 2048 | tf_op jit(solution)/shard_map/psum | solution.py:99
  652.5 1.5 cholesky.159
  657.1 1.9 collective-permute-start.30
  659.0 7.9 %collective-permute-start.35 = (f32[4,16,128]{2,1,0:T(8,128)S(1)}, f32[4,16,128]{2,1,0:T(8,128)S(1)}, u32[]{:S(2)}, u32[]{:S(2)}) collective-permute-start(f32[4,16,128]{2,1,0:T(8,128)S(1)} %fusion.2), channel_id=1, source_target_pairs={{3,0},{4,1},{5,2},{6,3},{7,4},{8,5},{9,6},{10,7},{11,8},{12,9},{13... | collective-permute-start | bytes 98312 | tf_op jit(solution)/shard_map/ppermute | solution.py:15
  666.9 1.9 collective-permute-start.34
  668.8 4.7 collective-permute-start.33
  673.5 3.5 collective-permute-start.32
  677.1 2.0 collective-permute-start.31
  679.1 6.8 collective-permute-done.31
  686.8 10.0 %fusion = f32[4,16,128]{2,1,0:T(8,128)} fusion(f32[4,16,128]{2,1,0:T(8,128)S(1)} %copy-done.1, f32[4,32,128,128]{3,2,1,0:T(8,128)} %param.12, f32[4,32,16,128]{3,2,1,0:T(8,128)S(1)} %bitcast.245, pred[4,32]{1,0:T(4,128)(4,1)S(1)} %get-tuple-element.12), kind=kOutput, calls=%fused_computation.7 | convolution fusion | flops 402923520 | bytes 9502848 | tf_op jit(solution)/shard_map/ikab,ikcb->ica/dot_general | solution.py:52
  (164 shorter events, 26.3 us)
Async XLA Ops:
  0.6 337.5 %copy-start = (f32[4,128,128]{2,1,0:T(8,128)S(1)}, f32[4,128,128]{2,1,0:T(8,128)}, u32[]{:S(2)}) copy-start(f32[4,128,128]{2,1,0:T(8,128)} %param.14) | copy-start | bytes 786436
  0.6 36.2 %collective-permute-start.5 = (f32[4,16,128]{2,1,0:T(8,128)}, f32[4,16,128]{2,1,0:T(8,128)S(1)}, u32[]{:S(2)}, u32[]{:S(2)}) collective-permute-start(f32[4,16,128]{2,1,0:T(8,128)} %param.15), channel_id=1, source_target_pairs={{3,0},{4,1},{5,2},{6,3},{7,4},{8,5},{9,6},{10,7},{11,8},{12,9},{13... | collective-permute-start | bytes 98312 | tf_op jit(solution)/shard_map/ppermute | solution.py:15
  9.4 27.4 %collective-permute-start.4 = (f32[4,16,128]{2,1,0:T(8,128)}, f32[4,16,128]{2,1,0:T(8,128)S(1)}, u32[]{:S(2)}, u32[]{:S(2)}) collective-permute-start(f32[4,16,128]{2,1,0:T(8,128)} %param.15), channel_id=1, source_target_pairs={{2,0},{3,1},{4,2},{5,3},{6,4},{7,5},{8,6},{9,7},{10,8},{11,9},{12,... | collective-permute-start | bytes 98312 | tf_op jit(solution)/shard_map/ppermute | solution.py:15
  11.5 25.4 %collective-permute-start.3 = (f32[4,16,128]{2,1,0:T(8,128)}, f32[4,16,128]{2,1,0:T(8,128)S(1)}, u32[]{:S(2)}, u32[]{:S(2)}) collective-permute-start(f32[4,16,128]{2,1,0:T(8,128)} %param.15), channel_id=1, source_target_pairs={{1,0},{2,1},{3,2},{4,3},{5,4},{6,5},{7,6},{8,7},{9,8},{10,9},{11,1... | collective-permute-start | bytes 98312 | tf_op jit(solution)/shard_map/ppermute | solution.py:15
  13.7 22.4 %collective-permute-start.2 = (f32[4,16,128]{2,1,0:T(8,128)}, f32[4,16,128]{2,1,0:T(8,128)S(1)}, u32[]{:S(2)}, u32[]{:S(2)}) collective-permute-start(f32[4,16,128]{2,1,0:T(8,128)} %param.15), channel_id=1, source_target_pairs={{0,1},{1,2},{2,3},{3,4},{4,5},{5,6},{6,7},{7,8},{8,9},{9,10},{10,1... | collective-permute-start | bytes 98312 | tf_op jit(solution)/shard_map/ppermute | solution.py:15
  17.1 9.7 %collective-permute-start = (f32[4,16,128]{2,1,0:T(8,128)}, f32[4,16,128]{2,1,0:T(8,128)S(1)}, u32[]{:S(2)}, u32[]{:S(2)}) collective-permute-start(f32[4,16,128]{2,1,0:T(8,128)} %param.15), channel_id=1, source_target_pairs={{0,3},{1,4},{2,5},{3,6},{4,7},{5,8},{6,9},{7,10},{8,11},{9,12},{10... | collective-permute-start | bytes 98312 | tf_op jit(solution)/shard_map/ppermute | solution.py:15
  21.6 25.4 %copy-start.1 = (f32[4,16,128]{2,1,0:T(8,128)S(1)}, f32[4,16,128]{2,1,0:T(8,128)}, u32[]{:S(2)}) copy-start(f32[4,16,128]{2,1,0:T(8,128)} %param.15) | copy-start | bytes 98308
  26.7 9.3 %collective-permute-start.1 = (f32[4,16,128]{2,1,0:T(8,128)}, f32[4,16,128]{2,1,0:T(8,128)S(1)}, u32[]{:S(2)}, u32[]{:S(2)}) collective-permute-start(f32[4,16,128]{2,1,0:T(8,128)} %param.15), channel_id=1, source_target_pairs={{0,2},{1,3},{2,4},{3,5},{4,6},{5,7},{6,8},{7,9},{8,10},{9,11},{10,... | collective-permute-start | bytes 98312 | tf_op jit(solution)/shard_map/ppermute | solution.py:15
  192.0 22.0 %collective-permute-start.6 = (f32[4,16,128]{2,1,0:T(8,128)S(1)}, f32[4,16,128]{2,1,0:T(8,128)S(1)}, u32[]{:S(2)}, u32[]{:S(2)}) collective-permute-start(f32[4,16,128]{2,1,0:T(8,128)S(1)} %fusion.7), channel_id=1, source_target_pairs={{0,3},{1,4},{2,5},{3,6},{4,7},{5,8},{6,9},{7,10},{8,11},{9,12},{10... | collective-permute-start | bytes 98312 | tf_op jit(solution)/shard_map/ppermute | solution.py:15
  194.1 28.9 %collective-permute-start.11 = (f32[4,16,128]{2,1,0:T(8,128)S(1)}, f32[4,16,128]{2,1,0:T(8,128)S(1)}, u32[]{:S(2)}, u32[]{:S(2)}) collective-permute-start(f32[4,16,128]{2,1,0:T(8,128)S(1)} %fusion.7), channel_id=1, source_target_pairs={{3,0},{4,1},{5,2},{6,3},{7,4},{8,5},{9,6},{10,7},{11,8},{12,9},{13... | collective-permute-start | bytes 98312 | tf_op jit(solution)/shard_map/ppermute | solution.py:15
  201.9 21.0 %collective-permute-start.10 = (f32[4,16,128]{2,1,0:T(8,128)S(1)}, f32[4,16,128]{2,1,0:T(8,128)S(1)}, u32[]{:S(2)}, u32[]{:S(2)}) collective-permute-start(f32[4,16,128]{2,1,0:T(8,128)S(1)} %fusion.7), channel_id=1, source_target_pairs={{2,0},{3,1},{4,2},{5,3},{6,4},{7,5},{8,6},{9,7},{10,8},{11,9},{12,... | collective-permute-start | bytes 98312 | tf_op jit(solution)/shard_map/ppermute | solution.py:15
  203.9 19.0 %collective-permute-start.9 = (f32[4,16,128]{2,1,0:T(8,128)S(1)}, f32[4,16,128]{2,1,0:T(8,128)S(1)}, u32[]{:S(2)}, u32[]{:S(2)}) collective-permute-start(f32[4,16,128]{2,1,0:T(8,128)S(1)} %fusion.7), channel_id=1, source_target_pairs={{1,0},{2,1},{3,2},{4,3},{5,4},{6,5},{7,6},{8,7},{9,8},{10,9},{11,1... | collective-permute-start | bytes 98312 | tf_op jit(solution)/shard_map/ppermute | solution.py:15
  210.4 12.4 %collective-permute-start.8 = (f32[4,16,128]{2,1,0:T(8,128)S(1)}, f32[4,16,128]{2,1,0:T(8,128)S(1)}, u32[]{:S(2)}, u32[]{:S(2)}) collective-permute-start(f32[4,16,128]{2,1,0:T(8,128)S(1)} %fusion.7), channel_id=1, source_target_pairs={{0,1},{1,2},{2,3},{3,4},{4,5},{5,6},{6,7},{7,8},{8,9},{9,10},{10,1... | collective-permute-start | bytes 98312 | tf_op jit(solution)/shard_map/ppermute | solution.py:15
  214.0 8.9 %collective-permute-start.7 = (f32[4,16,128]{2,1,0:T(8,128)S(1)}, f32[4,16,128]{2,1,0:T(8,128)S(1)}, u32[]{:S(2)}, u32[]{:S(2)}) collective-permute-start(f32[4,16,128]{2,1,0:T(8,128)S(1)} %fusion.7), channel_id=1, source_target_pairs={{0,2},{1,3},{2,4},{3,5},{4,6},{5,7},{6,8},{7,9},{8,10},{9,11},{10,... | collective-permute-start | bytes 98312 | tf_op jit(solution)/shard_map/ppermute | solution.py:15
  222.9 80.4 %copy-start.3 = (s32[4,32]{1,0:T(4,128)S(1)}, s32[4,32]{1,0:T(4,128)}, u32[]{:S(2)}) copy-start(s32[4,32]{1,0:T(4,128)} %param.13) | copy-start | bytes 1540
  299.7 18.8 %collective-permute-start.12 = (f32[4,16,128]{2,1,0:T(8,128)S(1)}, f32[4,16,128]{2,1,0:T(8,128)S(1)}, u32[]{:S(2)}, u32[]{:S(2)}) collective-permute-start(f32[4,16,128]{2,1,0:T(8,128)S(1)} %fusion.6), channel_id=1, source_target_pairs={{0,3},{1,4},{2,5},{3,6},{4,7},{5,8},{6,9},{7,10},{8,11},{9,12},{10... | collective-permute-start | bytes 98312 | tf_op jit(solution)/shard_map/ppermute | solution.py:15
  304.0 23.9 %collective-permute-start.17 = (f32[4,16,128]{2,1,0:T(8,128)S(1)}, f32[4,16,128]{2,1,0:T(8,128)S(1)}, u32[]{:S(2)}, u32[]{:S(2)}) collective-permute-start(f32[4,16,128]{2,1,0:T(8,128)S(1)} %fusion.6), channel_id=1, source_target_pairs={{3,0},{4,1},{5,2},{6,3},{7,4},{8,5},{9,6},{10,7},{11,8},{12,9},{13... | collective-permute-start | bytes 98312 | tf_op jit(solution)/shard_map/ppermute | solution.py:15
  310.1 17.7 %collective-permute-start.16 = (f32[4,16,128]{2,1,0:T(8,128)S(1)}, f32[4,16,128]{2,1,0:T(8,128)S(1)}, u32[]{:S(2)}, u32[]{:S(2)}) collective-permute-start(f32[4,16,128]{2,1,0:T(8,128)S(1)} %fusion.6), channel_id=1, source_target_pairs={{2,0},{3,1},{4,2},{5,3},{6,4},{7,5},{8,6},{9,7},{10,8},{11,9},{12,... | collective-permute-start | bytes 98312 | tf_op jit(solution)/shard_map/ppermute | solution.py:15
  312.7 15.2 %collective-permute-start.15 = (f32[4,16,128]{2,1,0:T(8,128)S(1)}, f32[4,16,128]{2,1,0:T(8,128)S(1)}, u32[]{:S(2)}, u32[]{:S(2)}) collective-permute-start(f32[4,16,128]{2,1,0:T(8,128)S(1)} %fusion.6), channel_id=1, source_target_pairs={{1,0},{2,1},{3,2},{4,3},{5,4},{6,5},{7,6},{8,7},{9,8},{10,9},{11,1... | collective-permute-start | bytes 98312 | tf_op jit(solution)/shard_map/ppermute | solution.py:15
  315.8 12.0 %collective-permute-start.14 = (f32[4,16,128]{2,1,0:T(8,128)S(1)}, f32[4,16,128]{2,1,0:T(8,128)S(1)}, u32[]{:S(2)}, u32[]{:S(2)}) collective-permute-start(f32[4,16,128]{2,1,0:T(8,128)S(1)} %fusion.6), channel_id=1, source_target_pairs={{0,1},{1,2},{2,3},{3,4},{4,5},{5,6},{6,7},{7,8},{8,9},{9,10},{10,1... | collective-permute-start | bytes 98312 | tf_op jit(solution)/shard_map/ppermute | solution.py:15
  318.5 9.3 %collective-permute-start.13 = (f32[4,16,128]{2,1,0:T(8,128)S(1)}, f32[4,16,128]{2,1,0:T(8,128)S(1)}, u32[]{:S(2)}, u32[]{:S(2)}) collective-permute-start(f32[4,16,128]{2,1,0:T(8,128)S(1)} %fusion.6), channel_id=1, source_target_pairs={{0,2},{1,3},{2,4},{3,5},{4,6},{5,7},{6,8},{7,9},{8,10},{9,11},{10,... | collective-permute-start | bytes 98312 | tf_op jit(solution)/shard_map/ppermute | solution.py:15
  338.6 10.8 %collective-permute-start.18 = (f32[4,16,128]{2,1,0:T(8,128)S(1)}, f32[4,16,128]{2,1,0:T(8,128)S(1)}, u32[]{:S(2)}, u32[]{:S(2)}) collective-permute-start(f32[4,16,128]{2,1,0:T(8,128)S(1)} %fusion.81), channel_id=1, source_target_pairs={{0,3},{1,4},{2,5},{3,6},{4,7},{5,8},{6,9},{7,10},{8,11},{9,12},{10... | collective-permute-start | bytes 98312 | tf_op jit(solution)/shard_map/ppermute | solution.py:15
  340.1 14.4 %collective-permute-start.23 = (f32[4,16,128]{2,1,0:T(8,128)S(1)}, f32[4,16,128]{2,1,0:T(8,128)S(1)}, u32[]{:S(2)}, u32[]{:S(2)}) collective-permute-start(f32[4,16,128]{2,1,0:T(8,128)S(1)} %fusion.81), channel_id=1, source_target_pairs={{3,0},{4,1},{5,2},{6,3},{7,4},{8,5},{9,6},{10,7},{11,8},{12,9},{13... | collective-permute-start | bytes 98312 | tf_op jit(solution)/shard_map/ppermute | solution.py:15
  341.4 13.0 %collective-permute-start.22 = (f32[4,16,128]{2,1,0:T(8,128)S(1)}, f32[4,16,128]{2,1,0:T(8,128)S(1)}, u32[]{:S(2)}, u32[]{:S(2)}) collective-permute-start(f32[4,16,128]{2,1,0:T(8,128)S(1)} %fusion.81), channel_id=1, source_target_pairs={{2,0},{3,1},{4,2},{5,3},{6,4},{7,5},{8,6},{9,7},{10,8},{11,9},{12,... | collective-permute-start | bytes 98312 | tf_op jit(solution)/shard_map/ppermute | solution.py:15
  342.7 11.7 %collective-permute-start.21 = (f32[4,16,128]{2,1,0:T(8,128)S(1)}, f32[4,16,128]{2,1,0:T(8,128)S(1)}, u32[]{:S(2)}, u32[]{:S(2)}) collective-permute-start(f32[4,16,128]{2,1,0:T(8,128)S(1)} %fusion.81), channel_id=1, source_target_pairs={{1,0},{2,1},{3,2},{4,3},{5,4},{6,5},{7,6},{8,7},{9,8},{10,9},{11,1... | collective-permute-start | bytes 98312 | tf_op jit(solution)/shard_map/ppermute | solution.py:15
  345.2 9.2 %collective-permute-start.20 = (f32[4,16,128]{2,1,0:T(8,128)S(1)}, f32[4,16,128]{2,1,0:T(8,128)S(1)}, u32[]{:S(2)}, u32[]{:S(2)}) collective-permute-start(f32[4,16,128]{2,1,0:T(8,128)S(1)} %fusion.81), channel_id=1, source_target_pairs={{0,1},{1,2},{2,3},{3,4},{4,5},{5,6},{6,7},{7,8},{8,9},{9,10},{10,1... | collective-permute-start | bytes 98312 | tf_op jit(solution)/shard_map/ppermute | solution.py:15
  349.4 5.0 collective-permute-start.19
  563.4 10.8 %collective-permute-start.24 = (f32[4,16,128]{2,1,0:T(8,128)S(1)}, f32[4,16,128]{2,1,0:T(8,128)S(1)}, u32[]{:S(2)}, u32[]{:S(2)}) collective-permute-start(f32[4,16,128]{2,1,0:T(8,128)S(1)} %fusion.3), channel_id=1, source_target_pairs={{0,3},{1,4},{2,5},{3,6},{4,7},{5,8},{6,9},{7,10},{8,11},{9,12},{10... | collective-permute-start | bytes 98312 | tf_op jit(solution)/shard_map/ppermute | solution.py:15
  564.9 14.5 %collective-permute-start.29 = (f32[4,16,128]{2,1,0:T(8,128)S(1)}, f32[4,16,128]{2,1,0:T(8,128)S(1)}, u32[]{:S(2)}, u32[]{:S(2)}) collective-permute-start(f32[4,16,128]{2,1,0:T(8,128)S(1)} %fusion.3), channel_id=1, source_target_pairs={{3,0},{4,1},{5,2},{6,3},{7,4},{8,5},{9,6},{10,7},{11,8},{12,9},{13... | collective-permute-start | bytes 98312 | tf_op jit(solution)/shard_map/ppermute | solution.py:15
  566.2 13.1 %collective-permute-start.28 = (f32[4,16,128]{2,1,0:T(8,128)S(1)}, f32[4,16,128]{2,1,0:T(8,128)S(1)}, u32[]{:S(2)}, u32[]{:S(2)}) collective-permute-start(f32[4,16,128]{2,1,0:T(8,128)S(1)} %fusion.3), channel_id=1, source_target_pairs={{2,0},{3,1},{4,2},{5,3},{6,4},{7,5},{8,6},{9,7},{10,8},{11,9},{12,... | collective-permute-start | bytes 98312 | tf_op jit(solution)/shard_map/ppermute | solution.py:15
  567.5 11.8 %collective-permute-start.27 = (f32[4,16,128]{2,1,0:T(8,128)S(1)}, f32[4,16,128]{2,1,0:T(8,128)S(1)}, u32[]{:S(2)}, u32[]{:S(2)}) collective-permute-start(f32[4,16,128]{2,1,0:T(8,128)S(1)} %fusion.3), channel_id=1, source_target_pairs={{1,0},{2,1},{3,2},{4,3},{5,4},{6,5},{7,6},{8,7},{9,8},{10,9},{11,1... | collective-permute-start | bytes 98312 | tf_op jit(solution)/shard_map/ppermute | solution.py:15
  570.1 9.2 %collective-permute-start.26 = (f32[4,16,128]{2,1,0:T(8,128)S(1)}, f32[4,16,128]{2,1,0:T(8,128)S(1)}, u32[]{:S(2)}, u32[]{:S(2)}) collective-permute-start(f32[4,16,128]{2,1,0:T(8,128)S(1)} %fusion.3), channel_id=1, source_target_pairs={{0,1},{1,2},{2,3},{3,4},{4,5},{5,6},{6,7},{7,8},{8,9},{9,10},{10,1... | collective-permute-start | bytes 98312 | tf_op jit(solution)/shard_map/ppermute | solution.py:15
  574.3 5.0 collective-permute-start.25
  657.1 39.7 %copy-start.2 = (f32[4,16,128]{2,1,0:T(8,128)}, f32[4,16,128]{2,1,0:T(8,128)S(1)}, u32[]{:S(2)}) copy-start(f32[4,16,128]{2,1,0:T(8,128)S(1)} %fusion.2) | copy-start | bytes 98308
  657.1 19.9 %collective-permute-start.30 = (f32[4,16,128]{2,1,0:T(8,128)S(1)}, f32[4,16,128]{2,1,0:T(8,128)S(1)}, u32[]{:S(2)}, u32[]{:S(2)}) collective-permute-start(f32[4,16,128]{2,1,0:T(8,128)S(1)} %fusion.2), channel_id=1, source_target_pairs={{0,3},{1,4},{2,5},{3,6},{4,7},{5,8},{6,9},{7,10},{8,11},{9,12},{10... | collective-permute-start | bytes 98312 | tf_op jit(solution)/shard_map/ppermute | solution.py:15
  659.0 27.0 %collective-permute-start.35 = (f32[4,16,128]{2,1,0:T(8,128)S(1)}, f32[4,16,128]{2,1,0:T(8,128)S(1)}, u32[]{:S(2)}, u32[]{:S(2)}) collective-permute-start(f32[4,16,128]{2,1,0:T(8,128)S(1)} %fusion.2), channel_id=1, source_target_pairs={{3,0},{4,1},{5,2},{6,3},{7,4},{8,5},{9,6},{10,7},{11,8},{12,9},{13... | collective-permute-start | bytes 98312 | tf_op jit(solution)/shard_map/ppermute | solution.py:15
  666.9 19.1 %collective-permute-start.34 = (f32[4,16,128]{2,1,0:T(8,128)S(1)}, f32[4,16,128]{2,1,0:T(8,128)S(1)}, u32[]{:S(2)}, u32[]{:S(2)}) collective-permute-start(f32[4,16,128]{2,1,0:T(8,128)S(1)} %fusion.2), channel_id=1, source_target_pairs={{2,0},{3,1},{4,2},{5,3},{6,4},{7,5},{8,6},{9,7},{10,8},{11,9},{12,... | collective-permute-start | bytes 98312 | tf_op jit(solution)/shard_map/ppermute | solution.py:15
  668.8 17.1 %collective-permute-start.33 = (f32[4,16,128]{2,1,0:T(8,128)S(1)}, f32[4,16,128]{2,1,0:T(8,128)S(1)}, u32[]{:S(2)}, u32[]{:S(2)}) collective-permute-start(f32[4,16,128]{2,1,0:T(8,128)S(1)} %fusion.2), channel_id=1, source_target_pairs={{1,0},{2,1},{3,2},{4,3},{5,4},{6,5},{7,6},{8,7},{9,8},{10,9},{11,1... | collective-permute-start | bytes 98312 | tf_op jit(solution)/shard_map/ppermute | solution.py:15
  673.5 12.4 %collective-permute-start.32 = (f32[4,16,128]{2,1,0:T(8,128)S(1)}, f32[4,16,128]{2,1,0:T(8,128)S(1)}, u32[]{:S(2)}, u32[]{:S(2)}) collective-permute-start(f32[4,16,128]{2,1,0:T(8,128)S(1)} %fusion.2), channel_id=1, source_target_pairs={{0,1},{1,2},{2,3},{3,4},{4,5},{5,6},{6,7},{7,8},{8,9},{9,10},{10,1... | collective-permute-start | bytes 98312 | tf_op jit(solution)/shard_map/ppermute | solution.py:15
  677.1 8.9 %collective-permute-start.31 = (f32[4,16,128]{2,1,0:T(8,128)S(1)}, f32[4,16,128]{2,1,0:T(8,128)S(1)}, u32[]{:S(2)}, u32[]{:S(2)}) collective-permute-start(f32[4,16,128]{2,1,0:T(8,128)S(1)} %fusion.2), channel_id=1, source_target_pairs={{0,2},{1,3},{2,4},{3,5},{4,6},{5,7},{6,8},{7,9},{8,10},{9,11},{10,... | collective-permute-start | bytes 98312 | tf_op jit(solution)/shard_map/ppermute | solution.py:15
